TPU v7x, 32 devices: a whole 2x2x4 slice. The times are simulated.
32 devices in a mesh: dp: 4 (over z), comp: 8 (over y, x, core).
Axes of the slice: x: 2, y: 2, z: 4, core: 2. Of those that a mesh axis runs over, the one named last changes fastest.
Arguments:
- vectors: bfloat16 [512, 256], P('dp'), may hold values from -8 to 8
- centers: float32 [128, 256], P('comp'), may hold values from -1.5 to 1.5
- factors: bfloat16 [128, 256, 256], P('comp', 'dp'), may hold values from -1 to 9.065873, as said below
- mixing: float32 [128], P('comp'), may hold values from 0.00234375 to 0.0234375
Outputs:
- new_factors: float32 [128, 256, 256], P('comp', 'dp')
- new_means: float32 [128, 256], P('comp')
- new_weights: float32 [128], P('comp')
- evidence: float32 [512], P('dp')
Inputs may be any that keep to these rules, and one draw needn't show every extreme that they name: `factors`: each component's 256 x 256 factor is lower triangular with a positive diagonal.
All inputs are finite; a program needn't handle non-finite values.
Results may differ from a plain program's by a relative error of at most 0.0003.
Values may be sent and summed in bfloat16 or wider, within the bound.
A program may use at most 64 MiB of HBM per device.

v0:
```python
import math

import jax
import jax.numpy as jnp
from jax import lax
from jax.sharding import PartitionSpec as P

anneal = 1.0
step_weight = 0.5
ridge_term = 0.01
normal_offset = 0.9189385332046727
exact_mode = lax.Precision.HIGHEST


def normalize(density, mixing, features):
    scores = anneal * (density + jnp.log(mixing)[:, None] - features * normal_offset)
    row_max = jnp.max(scores, axis=0)
    joined_max = lax.pmax(row_max, "comp")
    joined_total = lax.psum(jnp.sum(jnp.exp(scores - joined_max[None, :]), axis=0), "comp")
    shares = jnp.exp(scores - joined_max[None, :]) / joined_total[None, :]
    evidence = (joined_max + jnp.log(joined_total)) / anneal
    return (shares, evidence)


def refactor(pieces):
    scaled, moment_part = pieces
    identity = jnp.eye(scaled.shape[-1], dtype=jnp.float32)
    inverse = lax.linalg.triangular_solve(scaled, identity, left_side=True, lower=True)
    covariance = (
        jnp.dot(inverse, inverse.T, precision=exact_mode) + moment_part + ridge_term * identity
    )
    cholesky_factor = jnp.linalg.cholesky(covariance)
    return lax.linalg.triangular_solve(cholesky_factor, identity, left_side=True, lower=True)


def local(vectors, centers, factors, mixing):
    comp_count, row_count, features = factors.shape
    groups = lax.axis_size("dp")
    owned_count = comp_count // groups
    position = lax.axis_index("dp")
    row_start = position * row_count
    everyone = lax.all_gather(vectors, "dp", axis=0, tiled=True)
    vector_total = everyone.shape[0]
    block_rows = math.gcd(vector_total, 512)
    block_count = vector_total // block_rows
    shifted = jnp.einsum("krd,kd->kr", factors.astype(jnp.float32), centers, precision=exact_mode)
    diag_block = lax.dynamic_slice_in_dim(factors, row_start, row_count, 2).astype(jnp.float32)
    log_diag = jnp.sum(jnp.log(jnp.diagonal(diag_block, axis1=1, axis2=2)), axis=1)
    flattened = factors.reshape(comp_count * row_count, features)
    vector_blocks = everyone.reshape(block_count, block_rows, features)

    def density_block(vector_block):
        whitened = lax.dot_general(
            flattened, vector_block, (((1,), (1,)), ((), ())), preferred_element_type=jnp.float32
        )
        whitened = whitened.reshape(comp_count, row_count, -1) - shifted[:, :, None]
        return log_diag[:, None] - 0.5 * jnp.sum(whitened * whitened, axis=1)

    partial_density = (
        lax.map(density_block, vector_blocks).transpose(1, 0, 2).reshape(comp_count, vector_total)
    )
    density = lax.psum_scatter(partial_density, "dp", scatter_dimension=1, tiled=True)
    shares_local, evidence = normalize(density, mixing, features)
    shares_all = lax.all_gather(shares_local, "dp", axis=1, tiled=True)
    share_blocks = shares_all.reshape(comp_count, block_count, block_rows).transpose(1, 0, 2)

    def accumulate(running, inputs):
        first_sum, gram_sum = running
        vector_block, share_block = inputs
        wide_block = vector_block.astype(jnp.float32)
        first_sum = first_sum + jnp.dot(share_block, wide_block, precision=exact_mode)
        own_share = lax.dynamic_slice_in_dim(share_block, position * owned_count, owned_count, 0)
        weighted = own_share[:, None, :] * wide_block.T[None]
        weighted = weighted.reshape(owned_count * features, -1)
        gram_term = jnp.dot(weighted, wide_block, precision=exact_mode)
        return ((first_sum, gram_sum + gram_term), None)

    gram_start = jnp.zeros((owned_count * features, features), jnp.float32)
    first_start = jnp.zeros((comp_count, features), jnp.float32)
    (first_moment, gram_sum), unused = lax.scan(
        accumulate, (first_start, gram_start), (vector_blocks, share_blocks)
    )
    counts = jnp.sum(shares_all, axis=1)
    kept_share = (1.0 - step_weight) * mixing
    new_weights = kept_share + step_weight * counts / vector_total
    new_means = (
        kept_share[:, None] * centers + step_weight * first_moment / vector_total
    ) / new_weights[:, None]
    retained = kept_share / new_weights
    own_start = position * owned_count
    kept_own = lax.dynamic_slice_in_dim(kept_share, own_start, owned_count, 0)
    weight_own = lax.dynamic_slice_in_dim(new_weights, own_start, owned_count, 0)
    retained_own = lax.dynamic_slice_in_dim(retained, own_start, owned_count, 0)
    center_own = lax.dynamic_slice_in_dim(centers, own_start, owned_count, 0)
    mean_own = lax.dynamic_slice_in_dim(new_means, own_start, owned_count, 0)
    gram_own = gram_sum.reshape(owned_count, features, features)
    moment_part = (
        kept_own[:, None, None] * center_own[:, :, None] * center_own[:, None, :]
        + step_weight * gram_own / vector_total
    ) / weight_own[:, None, None] - mean_own[:, :, None] * mean_own[:, None, :]
    whole_factors = lax.all_to_all(
        factors.reshape(groups, owned_count, row_count, features),
        "dp",
        split_axis=0,
        concat_axis=2,
        tiled=True,
    )
    scaled = whole_factors[0].astype(jnp.float32) * lax.rsqrt(retained_own)[:, None, None]
    refreshed = lax.map(refactor, (scaled, moment_part))
    new_factors = lax.all_to_all(
        refreshed[None], "dp", split_axis=2, concat_axis=0, tiled=True
    ).reshape(comp_count, row_count, features)
    return (new_factors, new_means, new_weights, evidence)


def solution(mesh):
    return jax.shard_map(
        local,
        mesh=mesh,
        in_specs=(P("dp", None), P("comp", None), P("comp", "dp", None), P("comp")),
        out_specs=(P("comp", "dp", None), P("comp", None), P("comp"), P("dp")),
        check_vma=False,
    )
```

profile of v0, /device:TPU:24, one launch (start us, length us, event | category | flops | bytes accessed | tf_op | source)
XLA Modules:
  0.0 498.5 jit_solution(12718491995252667038)
XLA Ops:
  7.2 1.1 constant_dynamic-slice_fusion.6
  9.2 0.9 gather_fusion
  10.1 14.5 %all_gather.6 = bf16[512,256]{1,0:T(8,128)(2,1)S(1)} all-gather(bf16[128,256]{1,0:T(8,128)(2,1)S(1)} %copy-done), channel_id=1, replica_groups=mesh['dp'=4,'comp'=8] {'dp'}, dimensions={0}, use_global_device_ids=true | all-gather | bytes 327680 | tf_op jit(solution)/shard_map/all_gather | solution.py:42
  24.6 1.5 fusion.38
  26.1 1.5 multiply_reduce_fusion
  28.4 5.1 %all-to-all-start = ((bf16[4,4,64,256]{3,2,1,0:T(8,128)(2,1)}), bf16[4,4,64,256]{3,2,1,0:T(8,128)(2,1)S(1)}, u32[]{:S(2)}, u32[]{:S(2)}) async-start(bf16[4,4,64,256]{3,2,1,0:T(8,128)(2,1)} %bitcast.10), calls=%async_computation | async-start | bytes 1048576 | tf_op jit(solution)/shard_map/all_to_all | solution.py:101
  33.7 12.1 %reduce-scatter.2.cloned.1.call-done = f32[16,128]{1,0:T(8,128)} async-done(((f32[16,512]{1,0:T(8,128)}), f32[16,128]{1,0:T(8,128)}) %reduce-scatter.2.cloned.1.call-update) | async-done | bytes 8208 | tf_op jit(solution)/shard_map/reduce_scatter | solution.py:62
  46.6 11.8 %pmax.7 = f32[128]{0:T(128)S(1)} all-reduce(f32[128]{0:T(128)S(1)} %fusion.40), channel_id=1, replica_groups=mesh['dp'=4,'comp'=8] {'comp'}, use_global_device_ids=true, to_apply=%region_4.5 | all-reduce | flops 128 | bytes 1024 | tf_op jit(solution)/shard_map/pmax | solution.py:18
  58.4 0.8 fusion.42
  59.2 12.0 %psum.7 = f32[128]{0:T(128)S(1)} all-reduce(f32[128]{0:T(128)S(1)} %fusion.42), channel_id=1, replica_groups=mesh['dp'=4,'comp'=8] {'comp'}, use_global_device_ids=true, to_apply=%region_6.7 | all-reduce | flops 128 | bytes 1024 | tf_op jit(solution)/shard_map/psum | solution.py:19
  72.0 13.1 %all_gather.7 = f32[16,512]{1,0:T(8,128)S(1)} all-gather(f32[16,128]{1,0:T(8,128)S(1)} %fusion.41), channel_id=1, replica_groups=mesh['dp'=4,'comp'=8] {'dp'}, dimensions={1}, use_global_device_ids=true | all-gather | bytes 40960 | tf_op jit(solution)/shard_map/all_gather | solution.py:64
  85.8 1.3 fusion.29
  87.4 376.0 %while.27 = (s32[]{:T(128)}, f32[4,256,256]{2,0,1:T(4,128)}, f32[4,256,256]{2,1,0:T(8,128)S(1)}, f32[4,256,256]{2,1,0:T(8,128)S(1)}, s32[]{:T(128)}, /*index=5*/s32[]{:T(128)}, f32[]{:T(128)}, s32[]{:T(128)}, s32[]{:T(128)}) while((s32[]{:T(128)}, f32[4,256,256]{2,0,1:T(4,128)}, f32[4,256,256]{2,1,0:T(8,128)S(1)}, ...), condition=%wide.region_13.15_spmd, body=%wide.region_8.14_spmd.sunk | while | flops 554909952 | bytes 10815953 | solution.py:109
  87.7 4.1 while.28
  88.4 1.3 bitcast_dynamic-update-slice_fusion.4
  90.4 1.3 bitcast_dynamic-update-slice_fusion.4
  91.8 19.7 %custom-call.23 = f32[2,128,128]{1,2,0:T(8,128)S(1)} custom-call(f32[2,128,128]{2,1,0:T(8,128)S(1)} %get-tuple-element.234), custom_call_target="InvertDiagBlocksLowerTriangular" | custom-call | tf_op jit(solution)/shard_map/while/body/eval_jaxpr/triangular_solve/custom-call.0 | solution.py:28
  113.3 11.7 %cholesky.180 = f32[128,128]{1,0:T(8,128)S(1)} custom-call(f32[128,128]{1,0:T(8,128)S(1)} %cholesky.179), custom_call_target="Cholesky" | custom-call | tf_op jit(solution)/shard_map/while/body/eval_jaxpr/jit(cholesky)/cholesky | solution.py:32
  125.1 9.8 %custom-call.24 = f32[1,128,128]{1,2,0:T(8,128)S(1)} custom-call(f32[1,128,128]{2,1,0:T(8,128)S(1)} %get-tuple-element.235), custom_call_target="InvertDiagBlocksLowerTriangular" | custom-call | tf_op jit(solution)/shard_map/while/body/eval_jaxpr/jit(cholesky)/cholesky | solution.py:32
  135.3 11.7 %cholesky.182 = f32[128,128]{1,0:T(8,128)S(1)} custom-call(f32[128,128]{1,0:T(8,128)S(1)} %convolution_subtract_fusion.7), custom_call_target="Cholesky" | custom-call | tf_op jit(solution)/shard_map/while/body/eval_jaxpr/jit(cholesky)/cholesky | solution.py:32
  149.5 4.3 while.29
  150.2 1.3 dynamic-slice.18
  152.3 1.3 dynamic-slice.18
  153.8 19.7 %custom-call.25 = f32[2,128,128]{1,2,0:T(8,128)S(1)} custom-call(f32[2,128,128]{2,1,0:T(8,128)S(1)} %get-tuple-element.239), custom_call_target="InvertDiagBlocksLowerTriangular" | custom-call | tf_op jit(solution)/shard_map/while/body/eval_jaxpr/triangular_solve/custom-call.0 | solution.py:33
  174.8 6.7 %dynamic_update_slice.8 = f32[4,256,256]{2,0,1:T(4,128)} dynamic-update-slice(f32[4,256,256]{2,0,1:T(4,128)} %get-tuple-element.293, f32[1,256,256]{2,0,1:T(1,128)S(1)} %copy.73, s32[]{:T(128)} %get-tuple-element.292, s32[]{:T(128)} %constant.148.clone.1..sunk, s32[]{:T(128)} %constant.148.clone.1..sunk) | dynamic-update-slice | bytes 524292 | tf_op jit(solution)/shard_map/while/body/jit(dynamic_update_index_in_dim)/dynamic_update_slice | solution.py:109
  181.6 4.1 while.28
  182.3 1.3 bitcast_dynamic-update-slice_fusion.4
  184.4 1.3 bitcast_dynamic-update-slice_fusion.4
  185.7 19.7 %custom-call.23 = f32[2,128,128]{1,2,0:T(8,128)S(1)} custom-call(f32[2,128,128]{2,1,0:T(8,128)S(1)} %get-tuple-element.234), custom_call_target="InvertDiagBlocksLowerTriangular" | custom-call | tf_op jit(solution)/shard_map/while/body/eval_jaxpr/triangular_solve/custom-call.0 | solution.py:28
  207.2 11.7 %cholesky.180 = f32[128,128]{1,0:T(8,128)S(1)} custom-call(f32[128,128]{1,0:T(8,128)S(1)} %cholesky.179), custom_call_target="Cholesky" | custom-call | tf_op jit(solution)/shard_map/while/body/eval_jaxpr/jit(cholesky)/cholesky | solution.py:32
  219.0 9.8 %custom-call.24 = f32[1,128,128]{1,2,0:T(8,128)S(1)} custom-call(f32[1,128,128]{2,1,0:T(8,128)S(1)} %get-tuple-element.235), custom_call_target="InvertDiagBlocksLowerTriangular" | custom-call | tf_op jit(solution)/shard_map/while/body/eval_jaxpr/jit(cholesky)/cholesky | solution.py:32
  229.3 11.7 %cholesky.182 = f32[128,128]{1,0:T(8,128)S(1)} custom-call(f32[128,128]{1,0:T(8,128)S(1)} %convolution_subtract_fusion.7), custom_call_target="Cholesky" | custom-call | tf_op jit(solution)/shard_map/while/body/eval_jaxpr/jit(cholesky)/cholesky | solution.py:32
  243.4 4.3 while.29
  244.1 1.3 dynamic-slice.18
  246.3 1.3 dynamic-slice.18
  247.7 19.7 %custom-call.25 = f32[2,128,128]{1,2,0:T(8,128)S(1)} custom-call(f32[2,128,128]{2,1,0:T(8,128)S(1)} %get-tuple-element.239), custom_call_target="InvertDiagBlocksLowerTriangular" | custom-call | tf_op jit(solution)/shard_map/while/body/eval_jaxpr/triangular_solve/custom-call.0 | solution.py:33
  268.8 6.7 %dynamic_update_slice.8 = f32[4,256,256]{2,0,1:T(4,128)} dynamic-update-slice(f32[4,256,256]{2,0,1:T(4,128)} %get-tuple-element.293, f32[1,256,256]{2,0,1:T(1,128)S(1)} %copy.73, s32[]{:T(128)} %get-tuple-element.292, s32[]{:T(128)} %constant.148.clone.1..sunk, s32[]{:T(128)} %constant.148.clone.1..sunk) | dynamic-update-slice | bytes 524292 | tf_op jit(solution)/shard_map/while/body/jit(dynamic_update_index_in_dim)/dynamic_update_slice | solution.py:109
  275.6 4.1 while.28
  276.3 1.3 bitcast_dynamic-update-slice_fusion.4
  278.3 1.3 bitcast_dynamic-update-slice_fusion.4
  279.7 19.7 %custom-call.23 = f32[2,128,128]{1,2,0:T(8,128)S(1)} custom-call(f32[2,128,128]{2,1,0:T(8,128)S(1)} %get-tuple-element.234), custom_call_target="InvertDiagBlocksLowerTriangular" | custom-call | tf_op jit(solution)/shard_map/while/body/eval_jaxpr/triangular_solve/custom-call.0 | solution.py:28
  301.2 11.7 %cholesky.180 = f32[128,128]{1,0:T(8,128)S(1)} custom-call(f32[128,128]{1,0:T(8,128)S(1)} %cholesky.179), custom_call_target="Cholesky" | custom-call | tf_op jit(solution)/shard_map/while/body/eval_jaxpr/jit(cholesky)/cholesky | solution.py:32
  312.9 9.8 %custom-call.24 = f32[1,128,128]{1,2,0:T(8,128)S(1)} custom-call(f32[1,128,128]{2,1,0:T(8,128)S(1)} %get-tuple-element.235), custom_call_target="InvertDiagBlocksLowerTriangular" | custom-call | tf_op jit(solution)/shard_map/while/body/eval_jaxpr/jit(cholesky)/cholesky | solution.py:32
  323.2 11.7 %cholesky.182 = f32[128,128]{1,0:T(8,128)S(1)} custom-call(f32[128,128]{1,0:T(8,128)S(1)} %convolution_subtract_fusion.7), custom_call_target="Cholesky" | custom-call | tf_op jit(solution)/shard_map/while/body/eval_jaxpr/jit(cholesky)/cholesky | solution.py:32
  337.4 4.3 while.29
  338.1 1.3 dynamic-slice.18
  340.2 1.3 dynamic-slice.18
  341.7 19.7 %custom-call.25 = f32[2,128,128]{1,2,0:T(8,128)S(1)} custom-call(f32[2,128,128]{2,1,0:T(8,128)S(1)} %get-tuple-element.239), custom_call_target="InvertDiagBlocksLowerTriangular" | custom-call | tf_op jit(solution)/shard_map/while/body/eval_jaxpr/triangular_solve/custom-call.0 | solution.py:33
  362.7 6.7 %dynamic_update_slice.8 = f32[4,256,256]{2,0,1:T(4,128)} dynamic-update-slice(f32[4,256,256]{2,0,1:T(4,128)} %get-tuple-element.293, f32[1,256,256]{2,0,1:T(1,128)S(1)} %copy.73, s32[]{:T(128)} %get-tuple-element.292, s32[]{:T(128)} %constant.148.clone.1..sunk, s32[]{:T(128)} %constant.148.clone.1..sunk) | dynamic-update-slice | bytes 524292 | tf_op jit(solution)/shard_map/while/body/jit(dynamic_update_index_in_dim)/dynamic_update_slice | solution.py:109
  369.5 4.1 while.28
  370.2 1.3 bitcast_dynamic-update-slice_fusion.4
  372.3 1.3 bitcast_dynamic-update-slice_fusion.4
  373.6 19.7 %custom-call.23 = f32[2,128,128]{1,2,0:T(8,128)S(1)} custom-call(f32[2,128,128]{2,1,0:T(8,128)S(1)} %get-tuple-element.234), custom_call_target="InvertDiagBlocksLowerTriangular" | custom-call | tf_op jit(solution)/shard_map/while/body/eval_jaxpr/triangular_solve/custom-call.0 | solution.py:28
  395.1 11.7 %cholesky.180 = f32[128,128]{1,0:T(8,128)S(1)} custom-call(f32[128,128]{1,0:T(8,128)S(1)} %cholesky.179), custom_call_target="Cholesky" | custom-call | tf_op jit(solution)/shard_map/while/body/eval_jaxpr/jit(cholesky)/cholesky | solution.py:32
  406.9 9.8 %custom-call.24 = f32[1,128,128]{1,2,0:T(8,128)S(1)} custom-call(f32[1,128,128]{2,1,0:T(8,128)S(1)} %get-tuple-element.235), custom_call_target="InvertDiagBlocksLowerTriangular" | custom-call | tf_op jit(solution)/shard_map/while/body/eval_jaxpr/jit(cholesky)/cholesky | solution.py:32
  417.2 11.7 %cholesky.182 = f32[128,128]{1,0:T(8,128)S(1)} custom-call(f32[128,128]{1,0:T(8,128)S(1)} %convolution_subtract_fusion.7), custom_call_target="Cholesky" | custom-call | tf_op jit(solution)/shard_map/while/body/eval_jaxpr/jit(cholesky)/cholesky | solution.py:32
  431.3 4.3 while.29
  432.0 1.3 dynamic-slice.18
  434.2 1.3 dynamic-slice.18
  435.6 19.7 %custom-call.25 = f32[2,128,128]{1,2,0:T(8,128)S(1)} custom-call(f32[2,128,128]{2,1,0:T(8,128)S(1)} %get-tuple-element.239), custom_call_target="InvertDiagBlocksLowerTriangular" | custom-call | tf_op jit(solution)/shard_map/while/body/eval_jaxpr/triangular_solve/custom-call.0 | solution.py:33
  456.7 6.7 %dynamic_update_slice.8 = f32[4,256,256]{2,0,1:T(4,128)} dynamic-update-slice(f32[4,256,256]{2,0,1:T(4,128)} %get-tuple-element.293, f32[1,256,256]{2,0,1:T(1,128)S(1)} %copy.73, s32[]{:T(128)} %get-tuple-element.292, s32[]{:T(128)} %constant.148.clone.1..sunk, s32[]{:T(128)} %constant.148.clone.1..sunk) | dynamic-update-slice | bytes 524292 | tf_op jit(solution)/shard_map/while/body/jit(dynamic_update_index_in_dim)/dynamic_update_slice | solution.py:109
  463.4 6.4 %all-to-all-start.1 = ((f32[1,4,256,256]{3,1,0,2:T(4,128)}), f32[1,4,256,256]{3,1,0,2:T(4,128)S(1)}, u32[]{:S(2)}, u32[]{:S(2)}) async-start(f32[1,4,256,256]{3,1,0,2:T(4,128)} %bitcast.113), calls=%async_computation.2 | async-start | bytes 2097152 | tf_op jit(solution)/shard_map/all_to_all | solution.py:110
  470.3 20.2 %all-to-all-done.1 = f32[1,4,256,256]{3,1,0,2:T(4,128)S(1)} async-done(((f32[1,4,256,256]{3,1,0,2:T(4,128)}), f32[1,4,256,256]{3,1,0,2:T(4,128)S(1)}, u32[]{:S(2)}, u32[]{:S(2)}) %all-to-all-start.1) | async-done | bytes 1048608 | tf_op jit(solution)/shard_map/all_to_all | solution.py:110
  490.5 1.2 copy.43
  (212 shorter events, 35.6 us)
Async XLA Ops:
  7.2 38.6 %reduce-scatter.2.cloned.1.call-start = ((), (), s32[]{:S(2)}) async-start(), calls=%async_computation.3 | async-start | bytes 40960 | tf_op jit(solution)/shard_map/reduce_scatter | solution.py:62
  8.3 1.7 copy-start
  8.9 15.7 %copy-start.1 = (f32[16,256]{1,0:T(8,128)S(1)}, f32[16,256]{1,0:T(8,128)}, u32[]{:S(2)}) copy-start(f32[16,256]{1,0:T(8,128)} %param.9) | copy-start | bytes 49156
  26.1 7.4 %copy-start.3 = (f32[16]{0:T(128)S(1)}, f32[16]{0:T(128)}, u32[]{:S(2)}) copy-start(f32[16]{0:T(128)} %param.11) | copy-start | bytes 196
  28.4 58.7 %all-to-all-start = ((bf16[4,4,64,256]{3,2,1,0:T(8,128)(2,1)}), bf16[4,4,64,256]{3,2,1,0:T(8,128)(2,1)S(1)}, u32[]{:S(2)}, u32[]{:S(2)}) async-start(bf16[4,4,64,256]{3,2,1,0:T(8,128)(2,1)} %bitcast.10), calls=%async_computation | async-start | bytes 1048576 | tf_op jit(solution)/shard_map/all_to_all | solution.py:101
  85.2 1.9 copy-start.4
  85.5 1.6 copy-start.2
  463.4 27.2 %all-to-all-start.1 = ((f32[1,4,256,256]{3,1,0,2:T(4,128)}), f32[1,4,256,256]{3,1,0,2:T(4,128)S(1)}, u32[]{:S(2)}, u32[]{:S(2)}) async-start(f32[1,4,256,256]{3,1,0,2:T(4,128)} %bitcast.113), calls=%async_computation.2 | async-start | bytes 2097152 | tf_op jit(solution)/shard_map/all_to_all | solution.py:110
Sparse Core Ops, SparseCore 0:
  28.5 17.2 reduce-scatter.1
where the time goes:
time: 504 us; the launch traced here: 499 us
  other arithmetic  298 us (59%)
  local copies, waits for them, and re-layouts  67.7 us (13%)
  blocking collectives  51.4 us (10%)
  waiting for transfers between devices  32.3 us (6%)
  matrix products  16.2 us (3%)
  between operations  14.2 us (3%)
  starting transfers between devices  11.6 us (2%)
  loops' own time  6.73 us (1%)
    another operation x24, other arithmetic, refactor(): cholesky_factor = jnp.linalg.cholesky(covariance)  136 us
    another operation x8, other arithmetic, refactor(): lax.linalg.triangular_solve(cholesky_factor, identity, left_side=True, lo...  78.8 us
    another operation x12, other arithmetic, refactor(): lax.linalg.triangular_solve(scaled, identity, left_side=True, lower=True)  78.8 us
    dynamic_update_slice x8, local copies, waits for them, and re-layouts, local(): refreshed = lax.map(refactor, (scaled, moment_part))  27.8 us
    all_to_all x1, waiting for transfers between devices, local(): lax.all_to_all(refreshed[None], 'dp', split_axis=2, concat_axis=0, tiled=...  20.2 us
    another operation x40, local copies, waits for them, and re-layouts, refactor(): lax.linalg.triangular_solve(cholesky_factor, identity, left_side=True, lo...  16.9 us
    another operation x36, local copies, waits for them, and re-layouts, refactor(): lax.linalg.triangular_solve(scaled, identity, left_side=True, lower=True)  16.4 us
    all_gather x1, blocking collectives, local(): everyone = lax.all_gather(vectors, 'dp', axis=0, tiled=True)  14.5 us
  transfers between devices with their start and end apart: 3, of which 2 were waited for; matrix products, arithmetic and copies ran while one was open for 1% of the time, Pallas kernels for 0%

commit v1 on v0

v1 whole, which is shorter than its diff:
```python
import functools

import jax
import jax.numpy as jnp
from jax import lax
from jax.experimental import pallas as pl
from jax.experimental.pallas import tpu as pltpu
from jax.sharding import PartitionSpec as P

step_weight = 0.5
ridge_term = 0.01
normal_offset = 0.9189385332046727
panel_rows = 32
lanes = 128
sub = 8
f32 = jnp.float32
bf16 = jnp.bfloat16
both_inner = (((1,), (1,)), ((), ()))
both_outer = (((0,), (0,)), ((), ()))


def split3(value):
    high = value.astype(bf16)
    rest = value - high.astype(f32)
    middle = rest.astype(bf16)
    low = (rest - middle.astype(f32)).astype(bf16)
    return high, middle, low


def product3(left, right, dims, axis):
    lh, lm, ll = left
    rh, rm, rl = right
    return lax.dot_general(
        jnp.concatenate([lh, lh, lh, lm, lm, ll], axis=axis),
        jnp.concatenate([rh, rm, rl, rh, rm, rh], axis=axis),
        dims,
        preferred_element_type=f32,
    )


def diagonal_mask(size):
    return lax.broadcasted_iota(jnp.int32, (size, size), 0) == lax.broadcasted_iota(
        jnp.int32, (size, size), 1
    )


def whiten(factor, everyone, center):
    raw = lax.dot_general(factor, everyone, both_inner, preferred_element_type=f32)
    return raw - jnp.sum(factor.astype(f32) * center, axis=1, keepdims=True)


def score_row(factor, whitened, mix):
    size = factor.shape[0]
    diagonal = jnp.sum(jnp.where(diagonal_mask(size), factor.astype(f32), 0.0), axis=0, keepdims=True)
    log_det = jnp.sum(jnp.log(diagonal), axis=1, keepdims=True)
    density = log_det - 0.5 * jnp.sum(whitened * whitened, axis=0, keepdims=True)
    return density + jnp.log(mix) - size * normal_offset


def middle_matrix(factor, whitened, share, coef, retained):
    size = factor.shape[0]
    q = coef * jnp.sum(whitened * share, axis=1, keepdims=True)
    q_row = jnp.transpose(jnp.broadcast_to(q, (size, lanes)))[0:1, :]
    parts = split3(whitened * jnp.sqrt(coef * share))
    gram = product3(parts, parts, both_inner, 1)
    ridge = ridge_term * lax.dot_general(factor, factor, both_inner, preferred_element_type=f32)
    return jnp.where(diagonal_mask(size), retained, 0.0) + ridge + (gram - q * q_row)


def eliminate(tiles, offset):
    tiles = [list(row) for row in tiles]
    count = len(tiles)
    row_id = lax.broadcasted_iota(jnp.int32, (sub, lanes), 0)
    scales = []
    for chunk in range(count):
        columns = [
            [
                jnp.broadcast_to(
                    tiles[r][0][:, offset + chunk * sub + k : offset + chunk * sub + k + 1], (sub, lanes)
                )
                for r in range(chunk, count)
            ]
            for k in range(sub)
        ]
        scale = jnp.zeros((sub, lanes), f32)
        for k in range(sub):
            pivot = columns[k][0][k : k + 1, :]
            inverse = 1.0 / pivot
            scale = jnp.where(row_id == k, lax.rsqrt(pivot), scale)
            mult = [column * inverse for column in columns[k]]
            mult[0] = jnp.where(row_id > k, mult[0], 0.0)
            for later in range(k + 1, sub):
                row = columns[later][0][k : k + 1, :]
                columns[later] = [c - m * row for c, m in zip(columns[later], mult)]
            for t in range(len(tiles[chunk])):
                row = tiles[chunk][t][k : k + 1, :]
                for r in range(chunk, count):
                    tiles[r][t] = tiles[r][t] - mult[r - chunk] * row
        scales.append(scale)
    return [[tile * scale for tile in row] for row, scale in zip(tiles, scales)]


def factor_panel(panel, size, group, left_ref, right_ref):
    first = panel * panel_rows
    half = first // lanes
    width = size // lanes
    lead = (width - half) * lanes
    finished = []
    for g in range(group):
        tiles = [
            [
                left_ref[g, first + r * sub : first + (r + 1) * sub, t * lanes : (t + 1) * lanes]
                for t in range(half, width)
            ]
            + [
                right_ref[g, first + r * sub : first + (r + 1) * sub, t * lanes : (t + 1) * lanes]
                for t in range(half + 1)
            ]
            for r in range(panel_rows // sub)
        ]
        finished.append(tiles)
    finished = [eliminate(tiles, first - half * lanes) for tiles in finished]
    rows = [jnp.concatenate([jnp.concatenate(row, axis=1) for row in tiles], axis=0) for tiles in finished]
    after = first + panel_rows
    if after < size:
        for g in range(group):
            parts = split3(rows[g])
            update = product3([part[:, :lead] for part in parts], parts, both_outer, 0)
            update = update[after - half * lanes :, :]
            left_ref[g, after:, half * lanes :] -= update[:, :lead]
            right_ref[g, after:, : (half + 1) * lanes] -= update[:, lead:]
    return [row[:, lead:] for row in rows]


def score_kernel(factor_ref, everyone_ref, center_ref, mix_ref, score_ref, stat_ref):
    group = factor_ref.shape[0]
    everyone = everyone_ref[...]
    for g in range(group):
        factor = factor_ref[g]
        whitened = whiten(factor, everyone, center_ref[g : g + 1, :])
        score_ref[g : g + 1, :] = score_row(factor, whitened, mix_ref[g : g + 1, :])
    scores = score_ref[...]
    top = jnp.max(scores, axis=0, keepdims=True)
    stat_ref[0:1, :] = top
    stat_ref[1:2, :] = jnp.sum(jnp.exp(scores - top), axis=0, keepdims=True)


def update_kernel(
    factor_ref, everyone_ref, center_ref, mix_ref, score_ref, tops_ref, totals_ref,
    fresh_ref, mean_ref, weight_ref, evidence_ref, left_ref, right_ref,
):
    group, size, unused = factor_ref.shape
    everyone = everyone_ref[...]
    total_vectors = everyone.shape[0]
    tops = tops_ref[...]
    top = jnp.max(tops, axis=0, keepdims=True)
    total = jnp.sum(totals_ref[...] * jnp.exp(tops - top), axis=0, keepdims=True)
    evidence_ref[...] = top + jnp.log(total)
    shares = jnp.exp(score_ref[...] - top) / total
    counts = jnp.sum(shares, axis=1, keepdims=True)
    first_moment = sum(
        jnp.dot(part, everyone, preferred_element_type=f32) for part in split3(shares)
    )
    kept = (1.0 - step_weight) * mix_ref[...]
    weights = kept + step_weight * counts / total_vectors
    weight_ref[...] = weights
    mean_ref[...] = (kept * center_ref[...] + step_weight * first_moment / total_vectors) / weights
    retained = kept / weights
    coef = step_weight / (total_vectors * weights)
    for g in range(group):
        factor = factor_ref[g]
        whitened = whiten(factor, everyone, center_ref[g : g + 1, :])
        left_ref[g] = middle_matrix(
            factor, whitened, shares[g : g + 1, :], coef[g : g + 1, :], retained[g : g + 1, :]
        )
        right_ref[g] = factor.astype(f32)
    for panel in range(size // panel_rows):
        rows = factor_panel(panel, size, group, left_ref, right_ref)
        first = panel * panel_rows
        for g in range(group):
            filled = rows[g].shape[1]
            fresh_ref[g, first : first + panel_rows, :filled] = rows[g]
            if filled < size:
                fresh_ref[g, first : first + panel_rows, filled:] = jnp.zeros(
                    (panel_rows, size - filled), f32
                )


def local(vectors, centers, factors, mixing):
    comp_count, row_count, features = factors.shape
    groups = lax.axis_size("dp")
    owned = comp_count // groups
    position = lax.axis_index("dp")
    row_start = position * owned
    everyone = lax.all_gather(vectors, "dp", axis=0, tiled=True)
    total_vectors = everyone.shape[0]
    whole = lax.all_to_all(
        factors.reshape(groups, owned, row_count, features), "dp", split_axis=0, concat_axis=2, tiled=True
    ).reshape(owned, features, features)
    own_centers = lax.dynamic_slice_in_dim(centers, row_start, owned, 0)
    own_mixing = lax.dynamic_slice_in_dim(mixing, row_start, owned, 0)[:, None]
    params = pltpu.CompilerParams(vmem_limit_bytes=48 * 1024 * 1024)
    scores, stats = pl.pallas_call(
        score_kernel,
        out_shape=(
            jax.ShapeDtypeStruct((owned, total_vectors), f32),
            jax.ShapeDtypeStruct((2, total_vectors), f32),
        ),
        compiler_params=params,
    )(whole, everyone, own_centers, own_mixing)
    gathered = lax.all_gather(stats, ("dp", "comp"), axis=1)
    fresh, means, weights, evidence = pl.pallas_call(
        update_kernel,
        out_shape=(
            jax.ShapeDtypeStruct((owned, features, features), f32),
            jax.ShapeDtypeStruct((owned, features), f32),
            jax.ShapeDtypeStruct((owned, 1), f32),
            jax.ShapeDtypeStruct((1, total_vectors), f32),
        ),
        scratch_shapes=[pltpu.VMEM((owned, features, features), f32)] * 2,
        compiler_params=params,
    )(whole, everyone, own_centers, own_mixing, scores, gathered[0], gathered[1])
    new_factors = lax.all_to_all(
        fresh[None], "dp", split_axis=2, concat_axis=0, tiled=True
    ).reshape(comp_count, row_count, features)
    packed = jnp.concatenate([means, jnp.broadcast_to(weights, (owned, lanes))], axis=1)
    packed = lax.all_gather(packed, "dp", axis=0, tiled=True)
    count = vectors.shape[0]
    own_evidence = lax.dynamic_slice_in_dim(evidence[0], position * count, count, 0)
    return new_factors, packed[:, :features], packed[:, features], own_evidence


def solution(mesh):
    return jax.shard_map(
        local,
        mesh=mesh,
        in_specs=(P("dp", None), P("comp", None), P("comp", "dp", None), P("comp")),
        out_specs=(P("comp", "dp", None), P("comp", None), P("comp"), P("dp")),
        check_vma=False,
    )
```

time: 504 us -> 135 us (0.27)
  the two profiles are of different devices: /device:TPU:24 before, /device:TPU:0 now
where the time goes in v1:
time: 135 us; the launch traced here: 134 us
  blocking collectives  94.3 us (70%)
  Pallas kernels  23.4 us (17%)
  starting transfers between devices  9.98 us (7%)
  local copies, waits for them, and re-layouts  5.88 us (4%)
    all_gather x1, blocking collectives, local(): gathered = lax.all_gather(stats, ('dp', 'comp'), axis=1)  41.4 us
    all_gather x1, blocking collectives, local(): packed = lax.all_gather(packed, 'dp', axis=0, tiled=True)  31.7 us
    pallas_call x1, Pallas kernels, local(): pl.pallas_call(update_kernel, out_shape=(jax.ShapeDtypeStruct((owned, fea...  22.8 us
    all_gather x1, blocking collectives, local(): everyone = lax.all_gather(vectors, 'dp', axis=0, tiled=True)  21.3 us
    all_to_all x1, starting transfers between devices, local(): lax.all_to_all(factors.reshape(groups, owned, row_count, features), 'dp',...  6.46 us
    all_to_all x1, starting transfers between devices, local(): lax.all_to_all(fresh[None], 'dp', split_axis=2, concat_axis=0, tiled=True)  3.52 us
  transfers between devices with their start and end apart: 2, of which 0 were waited for; matrix products, arithmetic and copies ran while one was open for 2% of the time, Pallas kernels for 0%

profile of v1, /device:TPU:0, one launch (start us, length us, event | category | flops | bytes accessed | tf_op | source)
XLA Modules:
  0.0 134.4 jit_solution(11783943463429342916)
XLA Ops:
  0.6 0.0 copy-start
  0.6 0.0 copy-start.1
  0.7 6.5 %all-to-all-start = ((bf16[4,4,64,256]{3,2,1,0:T(8,128)(2,1)}), bf16[4,4,64,256]{3,2,1,0:T(8,128)(2,1)S(1)}, u32[]{:S(2)}, u32[]{:S(2)}) async-start(bf16[4,4,64,256]{3,2,1,0:T(8,128)(2,1)} %bitcast.22), calls=%async_computation | async-start | bytes 1048576 | tf_op jit(solution)/shard_map/all_to_all | solution.py:197
  7.1 0.0 copy-start.2
  7.1 0.7 copy-done.2
  7.8 0.1 dynamic-slice_bitcast_fusion.1
  7.8 0.1 copy.18.mix_ref
  7.9 0.0 copy-done.1
  7.9 21.3 %all_gather.12.everyone_ref = bf16[512,256]{1,0:T(8,128)(2,1)S(1)} all-gather(bf16[128,256]{1,0:T(8,128)(2,1)S(1)} %copy-done.1), channel_id=1, replica_groups=mesh['dp'=4,'comp'=8] {'dp'}, dimensions={0}, use_global_device_ids=true | all-gather | bytes 327680 | tf_op jit(solution)/shard_map/all_gather | solution.py:195
  29.2 0.0 copy-done
  29.2 0.0 all-to-all-done
  29.3 0.6 shard_map.75
  29.9 41.4 %all-gather = f32[2,16384]{1,0:T(2,128)S(1)} all-gather(f32[2,512]{1,0:T(2,128)S(1)} %get-tuple-element.11), channel_id=2, replica_groups=mesh['dp'=4,'comp'=8] {'dp','comp'}, dimensions={1}, use_global_device_ids=true | all-gather | bytes 135168 | tf_op jit(solution)/shard_map/all_gather | solution.py:211
  71.3 0.3 slice_reduce_fusion
  71.7 22.8 %shard_map.76 = (f32[4,256,256]{2,1,0:T(8,128)S(1)}, f32[4,256]{1,0:T(4,128)S(1)}, f32[4,1]{1,0:T(4,128)S(1)}, f32[1,512]{1,0:T(1,128)S(1)}) custom-call(bf16[4,256,256]{2,1,0:T(8,128)(2,1)S(1)} %bitcast.17, bf16[512,256]{1,0:T(8,128)(2,1)S(1)} %all_gather.12.everyone_ref, f32[4,256]{1,0:T(4,128)S(1)} %constant_dynamic-slice_fusion.center_ref, ...), custom_call_target="tpu_custom_call" | custom-call | tf_op jit(solution)/shard_map/pallas_call | solution.py:212
  94.5 1.6 %copy.19 = f32[1,4,256,256]{3,1,0,2:T(4,128)} copy(f32[1,4,256,256]{3,2,1,0:T(8,128)S(1)} %bitcast.18) | data formatting | bytes 2097152 | tf_op jit(solution)/shard_map/broadcast_in_dim | solution.py:224
  96.1 3.5 %all-to-all-start.1 = ((f32[1,4,256,256]{3,1,0,2:T(4,128)}), f32[1,4,256,256]{3,1,0,2:T(4,128)S(1)}, u32[]{:S(2)}, u32[]{:S(2)}) async-start(f32[1,4,256,256]{3,1,0,2:T(4,128)} %copy.19), calls=%async_computation.1 | async-start | bytes 2097152 | tf_op jit(solution)/shard_map/all_to_all | solution.py:223
  99.6 0.1 reduce.2
  99.8 0.1 broadcast_in_dim.16
  99.8 31.7 %all-gather.1 = f32[4,4,384]{2,1,0:T(4,128)S(1)} all-gather(f32[1,4,384]{2,1,0:T(4,128)S(1)} %maximum_bitcast_fusion), channel_id=1, replica_groups=mesh['dp'=4,'comp'=8] {'dp'}, dimensions={0}, use_global_device_ids=true | all-gather | bytes 30720 | tf_op jit(solution)/shard_map/all_gather | solution.py:227
  131.5 0.6 slice.20
  132.2 0.5 dynamic-slice_bitcast_fusion
  132.7 0.6 slice_reduce_fusion.2
  133.3 0.0 all-to-all-done.1
  133.3 1.2 copy.20
  (6 shorter events, 0.1 us)
Async XLA Ops:
  0.6 28.6 %copy-start = (f32[16,256]{1,0:T(8,128)S(1)}, f32[16,256]{1,0:T(8,128)}, u32[]{:S(2)}) copy-start(f32[16,256]{1,0:T(8,128)} %param.5) | copy-start | bytes 49156
  0.6 7.3 %copy-start.1 = (bf16[128,256]{1,0:T(8,128)(2,1)S(1)}, bf16[128,256]{1,0:T(8,128)(2,1)}, u32[]{:S(2)}) copy-start(bf16[128,256]{1,0:T(8,128)(2,1)} %param.4) | copy-start | bytes 196612
  0.7 28.6 %all-to-all-start = ((bf16[4,4,64,256]{3,2,1,0:T(8,128)(2,1)}), bf16[4,4,64,256]{3,2,1,0:T(8,128)(2,1)S(1)}, u32[]{:S(2)}, u32[]{:S(2)}) async-start(bf16[4,4,64,256]{3,2,1,0:T(8,128)(2,1)} %bitcast.22), calls=%async_computation | async-start | bytes 1048576 | tf_op jit(solution)/shard_map/all_to_all | solution.py:197
  7.1 0.7 copy-start.2
  96.1 37.2 %all-to-all-start.1 = ((f32[1,4,256,256]{3,1,0,2:T(4,128)}), f32[1,4,256,256]{3,1,0,2:T(4,128)S(1)}, u32[]{:S(2)}, u32[]{:S(2)}) async-start(f32[1,4,256,256]{3,1,0,2:T(4,128)} %copy.19), calls=%async_computation.1 | async-start | bytes 2097152 | tf_op jit(solution)/shard_map/all_to_all | solution.py:223

commit v2 on v1

--- a/solution.py
+++ b/solution.py
@@ -57,14 +57,13 @@
     return density + jnp.log(mix) - size * normal_offset
 
 
-def middle_matrix(factor, whitened, share, coef, retained):
-    size = factor.shape[0]
+def add_moment(left, whitened, share, coef, retained):
+    size = left.shape[0]
     q = coef * jnp.sum(whitened * share, axis=1, keepdims=True)
     q_row = jnp.transpose(jnp.broadcast_to(q, (size, lanes)))[0:1, :]
     parts = split3(whitened * jnp.sqrt(coef * share))
     gram = product3(parts, parts, both_inner, 1)
-    ridge = ridge_term * lax.dot_general(factor, factor, both_inner, preferred_element_type=f32)
-    return jnp.where(diagonal_mask(size), retained, 0.0) + ridge + (gram - q * q_row)
+    return jnp.where(diagonal_mask(size), retained, 0.0) + left + (gram - q * q_row)
 
 
 def eliminate(tiles, offset):
@@ -132,30 +131,113 @@
     return [row[:, lead:] for row in rows]
 
 
-def score_kernel(factor_ref, everyone_ref, center_ref, mix_ref, score_ref, stat_ref):
-    group = factor_ref.shape[0]
-    everyone = everyone_ref[...]
-    for g in range(group):
-        factor = factor_ref[g]
+def merge(slots_ref):
+    count = slots_ref.shape[0]
+    tops = [slots_ref[i, 0:1, :] for i in range(count)]
+    top = functools.reduce(jnp.maximum, tops)
+    return top, sum(slots_ref[i, 1:2, :] * jnp.exp(tops[i] - top) for i in range(count))
+
+
+def remote(source, target, send_sem, recv_sem, axis, peer):
+    return pltpu.make_async_remote_copy(
+        src_ref=source,
+        dst_ref=target,
+        send_sem=send_sem,
+        recv_sem=recv_sem,
+        device_id={axis: peer},
+        device_id_type=pl.DeviceIdType.MESH,
+    )
+
+
+def spread(groups, position, axis, kind, sends, receives, source_of, target):
+    copies = []
+    for step in range(1, groups):
+        peer = lax.rem(position + step, groups)
+        copy = remote(
+            source_of(peer), target, sends.at[kind, step], receives.at[kind, step], axis, peer
+        )
+        copy.start()
+        copies.append(copy)
+    return copies
+
+
+def finish(copies):
+    for copy in copies:
+        copy.wait()
+
+
+def step_kernel(
+    groups, comps,
+    vectors_ref, factors_ref, center_ref, mix_ref,
+    out_ref, packed_ref, evidence_ref,
+    everyone_ref, whole_ref, score_ref, white_ref, left_ref, right_ref, fresh_ref,
+    comp_slots, dp_slots, sends, receives, comp_sends, comp_receives, out_sends, out_receives,
+):
+    position = lax.axis_index("dp")
+    column = lax.axis_index("comp")
+    unused, group, rows, size = factors_ref.shape
+    local_vectors = vectors_ref.shape[0]
+    total_vectors = groups * local_vectors
+
+    barrier = pltpu.get_barrier_semaphore()
+    for axis, place, count in (("dp", position, groups), ("comp", column, comps)):
+        for step in range(1, count):
+            pl.semaphore_signal(
+                barrier, inc=1, device_id={axis: lax.rem(place + step, count)},
+                device_id_type=pl.DeviceIdType.MESH,
+            )
+    pl.semaphore_wait(barrier, groups + comps - 2)
+
+    vector_copies = spread(
+        groups, position, "dp", 0, sends, receives, lambda peer: vectors_ref, everyone_ref.at[position]
+    )
+    factor_copies = spread(
+        groups, position, "dp", 1, sends, receives,
+        lambda peer: factors_ref.at[peer], whole_ref.at[:, position],
+    )
+    everyone_ref[position] = vectors_ref[...]
+    for g in range(group):
+        whole_ref[g, position] = factors_ref[position, g]
+    for tile in range(1, size // lanes):
+        @pl.when((position + 1) * rows <= tile * lanes)
+        def clear():
+            out_ref[:, :, :, tile * lanes : (tile + 1) * lanes] = jnp.zeros(
+                (groups, group, rows, lanes), f32
+            )
+    finish(vector_copies)
+    finish(factor_copies)
+
+    everyone = everyone_ref[...].reshape(total_vectors, size)
+    for g in range(group):
+        factor = whole_ref[g].reshape(size, size)
         whitened = whiten(factor, everyone, center_ref[g : g + 1, :])
+        white_ref[g] = whitened
         score_ref[g : g + 1, :] = score_row(factor, whitened, mix_ref[g : g + 1, :])
     scores = score_ref[...]
     top = jnp.max(scores, axis=0, keepdims=True)
-    stat_ref[0:1, :] = top
-    stat_ref[1:2, :] = jnp.sum(jnp.exp(scores - top), axis=0, keepdims=True)
-
-
-def update_kernel(
-    factor_ref, everyone_ref, center_ref, mix_ref, score_ref, tops_ref, totals_ref,
-    fresh_ref, mean_ref, weight_ref, evidence_ref, left_ref, right_ref,
-):
-    group, size, unused = factor_ref.shape
-    everyone = everyone_ref[...]
-    total_vectors = everyone.shape[0]
-    tops = tops_ref[...]
-    top = jnp.max(tops, axis=0, keepdims=True)
-    total = jnp.sum(totals_ref[...] * jnp.exp(tops - top), axis=0, keepdims=True)
+    comp_slots[column, 0:1, :] = top
+    comp_slots[column, 1:2, :] = jnp.sum(jnp.exp(scores - top), axis=0, keepdims=True)
+    copies = spread(
+        comps, column, "comp", 0, comp_sends, comp_receives,
+        lambda peer: comp_slots.at[column], comp_slots.at[column],
+    )
+    for g in range(group):
+        factor = whole_ref[g].reshape(size, size)
+        left_ref[g] = ridge_term * lax.dot_general(
+            factor, factor, both_inner, preferred_element_type=f32
+        )
+        right_ref[g] = factor.astype(f32)
+    finish(copies)
+    top, total = merge(comp_slots)
+    dp_slots[position, 0:1, :] = top
+    dp_slots[position, 1:2, :] = total
+    finish(spread(
+        groups, position, "dp", 2, sends, receives,
+        lambda peer: dp_slots.at[position], dp_slots.at[position],
+    ))
+    top, total = merge(dp_slots)
     evidence_ref[...] = top + jnp.log(total)
+
     shares = jnp.exp(score_ref[...] - top) / total
     counts = jnp.sum(shares, axis=1, keepdims=True)
     first_moment = sum(
@@ -163,71 +245,108 @@
     )
     kept = (1.0 - step_weight) * mix_ref[...]
     weights = kept + step_weight * counts / total_vectors
-    weight_ref[...] = weights
-    mean_ref[...] = (kept * center_ref[...] + step_weight * first_moment / total_vectors) / weights
+    means = (kept * center_ref[...] + step_weight * first_moment / total_vectors) / weights
+    packed_ref[position] = jnp.concatenate([means, jnp.broadcast_to(weights, (group, lanes))], axis=1)
+    mean_copies = spread(
+        groups, position, "dp", 3, sends, receives,
+        lambda peer: packed_ref.at[position], packed_ref.at[position],
+    )
     retained = kept / weights
     coef = step_weight / (total_vectors * weights)
     for g in range(group):
-        factor = factor_ref[g]
-        whitened = whiten(factor, everyone, center_ref[g : g + 1, :])
-        left_ref[g] = middle_matrix(
-            factor, whitened, shares[g : g + 1, :], coef[g : g + 1, :], retained[g : g + 1, :]
+        left_ref[g] = add_moment(
+            left_ref[g], white_ref[g], shares[g : g + 1, :], coef[g : g + 1, :], retained[g : g + 1, :]
         )
-        right_ref[g] = factor.astype(f32)
+
+    def width(target):
+        return -(-(target + 1) * rows // lanes) * lanes
+
+    def result_copy(source, target):
+        return remote(
+            fresh_ref.at[:, target * rows : (target + 1) * rows, : width(target)],
+            out_ref.at[source, :, :, : width(target)],
+            out_sends.at[target], out_receives.at[source], "dp", target,
+        )
+
+    sent = 0
     for panel in range(size // panel_rows):
-        rows = factor_panel(panel, size, group, left_ref, right_ref)
+        done = factor_panel(panel, size, group, left_ref, right_ref)
         first = panel * panel_rows
         for g in range(group):
-            filled = rows[g].shape[1]
-            fresh_ref[g, first : first + panel_rows, :filled] = rows[g]
-            if filled < size:
-                fresh_ref[g, first : first + panel_rows, filled:] = jnp.zeros(
-                    (panel_rows, size - filled), f32
-                )
+            fresh_ref[g, first : first + panel_rows, : done[g].shape[1]] = done[g]
+        while (sent + 1) * rows <= first + panel_rows:
+            target = sent
+
+            @pl.when(position != target)
+            def send():
+                result_copy(position, target).start()
+
+            @pl.when(position == target)
+            def keep():
+                for g in range(group):
+                    out_ref[target, g, :, : width(target)] = fresh_ref[
+                        g, target * rows : (target + 1) * rows, : width(target)
+                    ]
+
+            sent += 1
+    for target in range(groups):
+        @pl.when(position != target)
+        def drain():
+            result_copy(position, target).wait_send()
+
+        @pl.when(position == target)
+        def collect():
+            for source in range(groups):
+                if source != target:
+                    result_copy(source, target).wait_recv()
+
+    finish(mean_copies)
 
 
 def local(vectors, centers, factors, mixing):
     comp_count, row_count, features = factors.shape
-    groups = lax.axis_size("dp")
+    groups, comps = lax.axis_size("dp"), lax.axis_size("comp")
     owned = comp_count // groups
     position = lax.axis_index("dp")
-    row_start = position * owned
-    everyone = lax.all_gather(vectors, "dp", axis=0, tiled=True)
-    total_vectors = everyone.shape[0]
-    whole = lax.all_to_all(
-        factors.reshape(groups, owned, row_count, features), "dp", split_axis=0, concat_axis=2, tiled=True
-    ).reshape(owned, features, features)
-    own_centers = lax.dynamic_slice_in_dim(centers, row_start, owned, 0)
-    own_mixing = lax.dynamic_slice_in_dim(mixing, row_start, owned, 0)[:, None]
-    params = pltpu.CompilerParams(vmem_limit_bytes=48 * 1024 * 1024)
-    scores, stats = pl.pallas_call(
-        score_kernel,
+    local_vectors = vectors.shape[0]
+    total_vectors = local_vectors * groups
+    own_centers = lax.dynamic_slice_in_dim(centers, position * owned, owned, 0)
+    own_mixing = lax.dynamic_slice_in_dim(mixing, position * owned, owned, 0)[:, None]
+    dma = pltpu.SemaphoreType.DMA
+    in_vmem = pl.BlockSpec(memory_space=pltpu.VMEM)
+    fresh, packed, evidence = pl.pallas_call(
+        functools.partial(step_kernel, groups, comps),
         out_shape=(
-            jax.ShapeDtypeStruct((owned, total_vectors), f32),
-            jax.ShapeDtypeStruct((2, total_vectors), f32),
-        ),
-        compiler_params=params,
-    )(whole, everyone, own_centers, own_mixing)
-    gathered = lax.all_gather(stats, ("dp", "comp"), axis=1)
-    fresh, means, weights, evidence = pl.pallas_call(
-        update_kernel,
-        out_shape=(
-            jax.ShapeDtypeStruct((owned, features, features), f32),
-            jax.ShapeDtypeStruct((owned, features), f32),
-            jax.ShapeDtypeStruct((owned, 1), f32),
+            jax.ShapeDtypeStruct((groups, owned, row_count, features), f32),
+            jax.ShapeDtypeStruct((groups, owned, features + lanes), f32),
             jax.ShapeDtypeStruct((1, total_vectors), f32),
         ),
-        scratch_shapes=[pltpu.VMEM((owned, features, features), f32)] * 2,
-        compiler_params=params,
-    )(whole, everyone, own_centers, own_mixing, scores, gathered[0], gathered[1])
-    new_factors = lax.all_to_all(
-        fresh[None], "dp", split_axis=2, concat_axis=0, tiled=True
-    ).reshape(comp_count, row_count, features)
-    packed = jnp.concatenate([means, jnp.broadcast_to(weights, (owned, lanes))], axis=1)
-    packed = lax.all_gather(packed, "dp", axis=0, tiled=True)
-    count = vectors.shape[0]
-    own_evidence = lax.dynamic_slice_in_dim(evidence[0], position * count, count, 0)
-    return new_factors, packed[:, :features], packed[:, features], own_evidence
+        in_specs=[in_vmem] * 4,
+        out_specs=(in_vmem,) * 3,
+        scratch_shapes=[
+            pltpu.VMEM((groups, local_vectors, features), bf16),
+            pltpu.VMEM((owned, groups, row_count, features), bf16),
+            pltpu.VMEM((owned, total_vectors), f32),
+            pltpu.VMEM((owned, features, total_vectors), f32),
+            pltpu.VMEM((owned, features, features), f32),
+            pltpu.VMEM((owned, features, features), f32),
+            pltpu.VMEM((owned, features, features), f32),
+            pltpu.VMEM((comps, 2, total_vectors), f32),
+            pltpu.VMEM((groups, 2, total_vectors), f32),
+            dma((4, groups)), dma((4, groups)),
+            dma((1, comps)), dma((1, comps)),
+            dma((groups,)), dma((groups,)),
+        ],
+        compiler_params=pltpu.CompilerParams(
+            collective_id=0, has_side_effects=True, vmem_limit_bytes=48 * 1024 * 1024
+        ),
+    )(vectors, factors.reshape(groups, owned, row_count, features), own_centers, own_mixing)
+    packed = packed.reshape(comp_count, features + lanes)
+    own_evidence = lax.dynamic_slice_in_dim(evidence[0], position * local_vectors, local_vectors, 0)
+    return (
+        fresh.reshape(comp_count, row_count, features),
+        packed[:, :features], packed[:, features], own_evidence,
+    )
 
 
 def solution(mesh):

time: 135 us -> 78.2 us (0.58)
  the two profiles are of different devices: /device:TPU:0 before, /device:TPU:24 now
where the time goes in v2:
time: 78.2 us; the launch traced here: 78 us
  Pallas kernels  71.2 us (91%)
  local copies, waits for them, and re-layouts  6.15 us (8%)
    pallas_call x1, Pallas kernels, local(): pl.pallas_call(functools.partial(step_kernel, groups, comps), out_shape=(...  71.2 us
    unnamed x9, local copies, waits for them, and re-layouts  4.21 us

profile of v2, /device:TPU:24, one launch (start us, length us, event | category | flops | bytes accessed | tf_op | source)
XLA Modules:
  0.0 78.0 jit_solution(6065252517894883628)
XLA Ops:
  0.6 0.0 copy-start
  0.7 0.7 copy-done
  1.4 0.0 copy-start.3
  1.4 0.6 copy-done.3
  2.0 0.1 dynamic-slice_bitcast_fusion.1
  2.1 0.1 copy.9.mix_ref
  2.2 0.0 copy-start.1
  2.2 1.0 %copy-done.1 = bf16[16,64,256]{2,1,0:T(8,128)(2,1)S(1)} copy-done((bf16[16,64,256]{2,1,0:T(8,128)(2,1)S(1)}, bf16[16,64,256]{2,1,0:T(8,128)(2,1)}, u32[]{:S(2)}) %copy-start.1) | copy-done | bytes 524312
  3.2 0.0 copy-start.2
  3.2 0.8 %copy-done.2 = bf16[128,256]{1,0:T(8,128)(2,1)S(1)} copy-done((bf16[128,256]{1,0:T(8,128)(2,1)S(1)}, bf16[128,256]{1,0:T(8,128)(2,1)}, u32[]{:S(2)}) %copy-start.2) | copy-done | bytes 65560
  4.1 71.2 %shard_map.75 = (f32[4,4,64,256]{3,2,1,0:T(8,128)S(1)}, f32[4,4,384]{2,1,0:T(4,128)S(1)}, f32[1,512]{1,0:T(1,128)S(1)}) custom-call(bf16[128,256]{1,0:T(8,128)(2,1)S(1)} %copy-done.2, bf16[4,4,64,256]{3,2,1,0:T(8,128)(2,1)S(1)} %bitcast.7, f32[4,256]{1,0:T(4,128)S(1)} %constant_dynamic-slice_fusion.center_ref, f32[4,1]{1,0:T(4,128)S(1)} %copy.9.mix_ref), custom_call_target="tpu_custom_call" | custom-call | tf_op jit(solution)/shard_map/pallas_call | solution.py:317
  75.2 0.5 dynamic-slice_bitcast_fusion
  75.8 0.6 slice.8
  76.4 0.6 slice_reduce_fusion
  77.0 1.0 %copy.11 = f32[16,64,256]{2,1,0:T(8,128)} copy(f32[16,64,256]{2,1,0:T(8,128)S(1)} %bitcast.6) | data formatting | bytes 2097152
  (2 shorter events, 0.0 us)
Async XLA Ops:
  0.6 0.7 copy-start
  1.4 0.7 copy-start.3
  2.2 1.0 %copy-start.1 = (bf16[16,64,256]{2,1,0:T(8,128)(2,1)S(1)}, bf16[16,64,256]{2,1,0:T(8,128)(2,1)}, u32[]{:S(2)}) copy-start(bf16[16,64,256]{2,1,0:T(8,128)(2,1)} %param.6) | copy-start | bytes 1572868
  3.2 0.8 %copy-start.2 = (bf16[128,256]{1,0:T(8,128)(2,1)S(1)}, bf16[128,256]{1,0:T(8,128)(2,1)}, u32[]{:S(2)}) copy-start(bf16[128,256]{1,0:T(8,128)(2,1)} %vectors_ref.1) | copy-start | bytes 196612

commit v3 on v2

--- a/solution.py
+++ b/solution.py
@@ -261,11 +261,15 @@
     def width(target):
         return -(-(target + 1) * rows // lanes) * lanes
 
-    def result_copy(source, target):
+    unit = min(panel_rows, rows)
+    pieces = rows // unit
+
+    def result_copy(source, target, piece):
+        start = target * rows + piece * unit
         return remote(
-            fresh_ref.at[:, target * rows : (target + 1) * rows, : width(target)],
-            out_ref.at[source, :, :, : width(target)],
-            out_sends.at[target], out_receives.at[source], "dp", target,
+            fresh_ref.at[:, start : start + unit, : width(target)],
+            out_ref.at[source, :, piece * unit : (piece + 1) * unit, : width(target)],
+            out_sends.at[target, piece], out_receives.at[source, piece], "dp", target,
         )
 
     sent = 0
@@ -274,31 +278,34 @@
         first = panel * panel_rows
         for g in range(group):
             fresh_ref[g, first : first + panel_rows, : done[g].shape[1]] = done[g]
-        while (sent + 1) * rows <= first + panel_rows:
-            target = sent
+        while (sent + 1) * unit <= first + panel_rows:
+            target, piece = divmod(sent, pieces)
+            start = sent * unit
 
             @pl.when(position != target)
             def send():
-                result_copy(position, target).start()
+                result_copy(position, target, piece).start()
 
             @pl.when(position == target)
             def keep():
                 for g in range(group):
-                    out_ref[target, g, :, : width(target)] = fresh_ref[
-                        g, target * rows : (target + 1) * rows, : width(target)
+                    out_ref[target, g, piece * unit : (piece + 1) * unit, : width(target)] = fresh_ref[
+                        g, start : start + unit, : width(target)
                     ]
 
             sent += 1
     for target in range(groups):
         @pl.when(position != target)
         def drain():
-            result_copy(position, target).wait_send()
+            for piece in range(pieces):
+                result_copy(position, target, piece).wait_send()
 
         @pl.when(position == target)
         def collect():
             for source in range(groups):
                 if source != target:
-                    result_copy(source, target).wait_recv()
+                    for piece in range(pieces):
+                        result_copy(source, target, piece).wait_recv()
 
     finish(mean_copies)
 
@@ -335,7 +342,8 @@
             pltpu.VMEM((groups, 2, total_vectors), f32),
             dma((4, groups)), dma((4, groups)),
             dma((1, comps)), dma((1, comps)),
-            dma((groups,)), dma((groups,)),
+            dma((groups, row_count // min(panel_rows, row_count))),
+            dma((groups, row_count // min(panel_rows, row_count))),
         ],
         compiler_params=pltpu.CompilerParams(
             collective_id=0, has_side_effects=True, vmem_limit_bytes=48 * 1024 * 1024

time: 78.2 us -> 76.8 us (0.982)
  Pallas kernels: 71.2 us -> 69.7 us
    pallas_call x1, Pallas kernels: 71.2 us -> 69.7 us  [local(): pl.pallas_call(functools.partial(step_kernel, groups, comps), out_shape=(...]
where the time goes in v3:
time: 76.8 us; the launch traced here: 76.6 us
  Pallas kernels  69.7 us (91%)
  local copies, waits for them, and re-layouts  6.15 us (8%)
    pallas_call x1, Pallas kernels, local(): pl.pallas_call(functools.partial(step_kernel, groups, comps), out_shape=(...  69.7 us
    unnamed x9, local copies, waits for them, and re-layouts  4.21 us

profile of v3, /device:TPU:24, one launch (start us, length us, event | category | flops | bytes accessed | tf_op | source)
XLA Modules:
  0.0 76.6 jit_solution(4104156027329431065)
XLA Ops:
  0.6 0.0 copy-start
  0.7 0.7 copy-done
  1.4 0.0 copy-start.3
  1.4 0.6 copy-done.3
  2.0 0.1 dynamic-slice_bitcast_fusion.1
  2.1 0.1 copy.9.mix_ref
  2.2 0.0 copy-start.1
  2.2 1.0 %copy-done.1 = bf16[16,64,256]{2,1,0:T(8,128)(2,1)S(1)} copy-done((bf16[16,64,256]{2,1,0:T(8,128)(2,1)S(1)}, bf16[16,64,256]{2,1,0:T(8,128)(2,1)}, u32[]{:S(2)}) %copy-start.1) | copy-done | bytes 524312
  3.2 0.0 copy-start.2
  3.2 0.8 %copy-done.2 = bf16[128,256]{1,0:T(8,128)(2,1)S(1)} copy-done((bf16[128,256]{1,0:T(8,128)(2,1)S(1)}, bf16[128,256]{1,0:T(8,128)(2,1)}, u32[]{:S(2)}) %copy-start.2) | copy-done | bytes 65560
  4.1 69.7 %shard_map.75 = (f32[4,4,64,256]{3,2,1,0:T(8,128)S(1)}, f32[4,4,384]{2,1,0:T(4,128)S(1)}, f32[1,512]{1,0:T(1,128)S(1)}) custom-call(bf16[128,256]{1,0:T(8,128)(2,1)S(1)} %copy-done.2, bf16[4,4,64,256]{3,2,1,0:T(8,128)(2,1)S(1)} %bitcast.7, f32[4,256]{1,0:T(4,128)S(1)} %constant_dynamic-slice_fusion.center_ref, f32[4,1]{1,0:T(4,128)S(1)} %copy.9.mix_ref), custom_call_target="tpu_custom_call" | custom-call | tf_op jit(solution)/shard_map/pallas_call | solution.py:324
  73.8 0.5 dynamic-slice_bitcast_fusion
  74.3 0.6 slice.8
  75.0 0.6 slice_reduce_fusion
  75.6 1.0 %copy.11 = f32[16,64,256]{2,1,0:T(8,128)} copy(f32[16,64,256]{2,1,0:T(8,128)S(1)} %bitcast.6) | data formatting | bytes 2097152
  (2 shorter events, 0.0 us)
Async XLA Ops:
  0.6 0.7 copy-start
  1.4 0.7 copy-start.3
  2.2 1.0 %copy-start.1 = (bf16[16,64,256]{2,1,0:T(8,128)(2,1)S(1)}, bf16[16,64,256]{2,1,0:T(8,128)(2,1)}, u32[]{:S(2)}) copy-start(bf16[16,64,256]{2,1,0:T(8,128)(2,1)} %param.6) | copy-start | bytes 1572868
  3.2 0.8 %copy-start.2 = (bf16[128,256]{1,0:T(8,128)(2,1)S(1)}, bf16[128,256]{1,0:T(8,128)(2,1)}, u32[]{:S(2)}) copy-start(bf16[128,256]{1,0:T(8,128)(2,1)} %vectors_ref.1) | copy-start | bytes 196612
